TPU v7x, 256 devices: a whole 4x4x8 slice. The times are simulated.
256 devices in a mesh: row: 64 (over z, x_lo, y), col: 4 (over x_hi, core).
Axes of the slice: x: 4 (x_hi: 2, x_lo: 2; x = x_hi * 2 + x_lo), y: 4, z: 8, core: 2. Of those that a mesh axis runs over, the one named last changes fastest.
Arguments:
- pair: bfloat16 [768, 768, 128], P('row', 'col'), may hold values from -6 to 6
- residue_mask: int32 [768], replicated, may hold values 0 or 1
- in_gain: float32 [2, 128], replicated, may hold values from 0.5 to 2
- w_in: bfloat16 [2, 5, 128, 128], replicated, may hold values from -0.5 to 0.5
- out_gain: float32 [2, 128], replicated, may hold values from 0.5 to 2
- w_out: bfloat16 [2, 128, 128], replicated, may hold values from -0.5 to 0.5
Outputs:
- pair_out: bfloat16 [768, 768, 128], P('row', 'col')
All inputs are finite; a program needn't handle non-finite values.
Results may differ from a plain program's by a relative error of at most 0.02.
Values may be sent and summed in bfloat16 or wider, within the bound.
A program may use at most 64 MiB of HBM per device.

v0:
```python
import jax
import jax.numpy as jnp
from jax import lax
from jax.sharding import PartitionSpec as P


def layer_norm(values, gain, axis_index):
    center = jnp.mean(values, axis=axis_index, keepdims=True)
    shifted = values - center
    spread = jnp.mean(shifted * shifted, axis=axis_index, keepdims=True)
    return shifted * lax.rsqrt(spread + 1e-05) * gain


def one_update(state, pair_mask, gain_in, weights_in, gain_out, weight_out, outgoing):
    normed = layer_norm(state.astype(jnp.float32), gain_in, -1).astype(jnp.bfloat16)
    projected = jnp.einsum("rjc,vcd->vdrj", normed, weights_in, preferred_element_type=jnp.float32)
    left_side = (jax.nn.sigmoid(projected[0]) * projected[1] * pair_mask).astype(jnp.bfloat16)
    right_side = (jax.nn.sigmoid(projected[2]) * projected[3] * pair_mask).astype(jnp.bfloat16)
    gate_vals = jax.nn.sigmoid(projected[4])
    left_side, right_side = (
        lax.all_to_all(left_side, "row", split_axis=0, concat_axis=1, tiled=True),
        lax.all_to_all(right_side, "row", split_axis=0, concat_axis=1, tiled=True),
    )
    if outgoing:
        summed = lax.psum_scatter(
            jnp.einsum(
                "cik,cjk->jci", left_side, right_side, preferred_element_type=jnp.float32
            ).astype(jnp.bfloat16),
            "col",
            scatter_dimension=0,
            tiled=True,
        )
        product = summed.transpose(1, 2, 0)
    else:
        product = jnp.einsum(
            "cki,ckj->cij",
            lax.all_gather(left_side, "col", axis=2, tiled=True),
            right_side,
            preferred_element_type=jnp.float32,
        ).astype(jnp.bfloat16)
    product = lax.all_to_all(product, "row", split_axis=1, concat_axis=0, tiled=True)
    tri_normed = layer_norm(product.astype(jnp.float32), gain_out[:, None, None], 0).astype(
        jnp.bfloat16
    )
    update_term = (
        jnp.einsum("crj,cd->drj", tri_normed, weight_out, preferred_element_type=jnp.float32)
        * gate_vals
    )
    result = state.astype(jnp.float32) + update_term.transpose(1, 2, 0)
    return result.astype(jnp.bfloat16)


def on_device(pair, residue_mask, in_gain, w_in, out_gain, w_out):
    row_count = pair.shape[0]
    col_count = pair.shape[1]
    row_mask = lax.dynamic_slice_in_dim(
        residue_mask, lax.axis_index("row") * row_count, row_count
    ).astype(jnp.float32)
    col_mask = lax.dynamic_slice_in_dim(
        residue_mask, lax.axis_index("col") * col_count, col_count
    ).astype(jnp.float32)
    pair_mask = row_mask[:, None] * col_mask[None, :]
    first = one_update(pair, pair_mask, in_gain[0], w_in[0], out_gain[0], w_out[0], True)
    return one_update(first, pair_mask, in_gain[1], w_in[1], out_gain[1], w_out[1], False)


def solution(mesh):
    placed = (P("row", "col", None), P(), P(), P(), P(), P())
    return jax.shard_map(
        on_device, mesh=mesh, in_specs=placed, out_specs=P("row", "col", None), check_vma=False
    )
```

profile of v0, /device:TPU:32, one launch (start us, length us, event | category | flops | bytes accessed | tf_op | source)
XLA Modules:
  0.0 308.6 jit_solution(131201018665595082)
XLA Ops:
  8.9 1.3 convert_reduce_fusion.1
  10.3 1.9 fusion.27
  12.2 1.1 convolution_bitcast_fusion.1
  14.1 1.8 copy-done.1
  15.9 1.9 copy.53
  17.8 12.7 %all-to-all-start = ((bf16[128,12,192]{2,1,0:T(8,128)(2,1)}), bf16[128,12,192]{2,1,0:T(8,128)(2,1)S(1)}, u32[]{:S(2)}, u32[]{:S(2)}) async-start(bf16[128,12,192]{2,1,0:T(8,128)(2,1)} %copy.53), calls=%async_computation | async-start | bytes 2097152 | tf_op jit(solution)/shard_map/all_to_all | solution.py:22
  30.5 1.9 copy.58
  32.5 25.6 %all-to-all-done = bf16[128,12,192]{2,1,0:T(8,128)(2,1)S(1)} async-done(((bf16[128,12,192]{2,1,0:T(8,128)(2,1)}), bf16[128,12,192]{2,1,0:T(8,128)(2,1)S(1)}, u32[]{:S(2)}, u32[]{:S(2)}) %all-to-all-start) | async-done | bytes 589856 | tf_op jit(solution)/shard_map/all_to_all | solution.py:22
  58.1 7.2 %all-to-all-start.1 = ((bf16[128,12,192]{2,1,0:T(8,128)(2,1)}), bf16[128,12,192]{2,1,0:T(8,128)(2,1)S(1)}, u32[]{:S(2)}, u32[]{:S(2)}) async-start(bf16[128,12,192]{2,1,0:T(8,128)(2,1)} %copy.58), calls=%async_computation.1 | async-start | bytes 2097152 | tf_op jit(solution)/shard_map/all_to_all | solution.py:21
  66.0 25.9 %all-to-all-done.1 = bf16[128,12,192]{2,1,0:T(8,128)(2,1)S(1)} async-done(((bf16[128,12,192]{2,1,0:T(8,128)(2,1)}), bf16[128,12,192]{2,1,0:T(8,128)(2,1)S(1)}, u32[]{:S(2)}, u32[]{:S(2)}) %all-to-all-start.1) | async-done | bytes 589856 | tf_op jit(solution)/shard_map/all_to_all | solution.py:21
  92.5 2.2 convert_bitcast_fusion
  94.7 43.0 %reduce-scatter.2.cloned.1.call-done = bf16[192,2,768]{2,0,1:T(8,128)(2,1)} async-done(((bf16[768,2,768]{2,0,1:T(8,128)(2,1)}), bf16[192,2,768]{2,0,1:T(8,128)(2,1)}) %reduce-scatter.2.cloned.1.call-update) | async-done | bytes 589840 | tf_op jit(solution)/shard_map/reduce_scatter | solution.py:25
  137.8 3.0 copy.63
  140.7 10.5 %all-to-all-start.2 = ((bf16[2,768,192]{2,0,1:T(2,128)(2,1)}), bf16[2,768,192]{2,0,1:T(2,128)(2,1)S(1)}, u32[]{:S(2)}, u32[]{:S(2)}) async-start(bf16[2,768,192]{2,0,1:T(2,128)(2,1)} %copy.63), calls=%async_computation.3 | async-start | bytes 1572864 | tf_op jit(solution)/shard_map/all_to_all | solution.py:41
  151.6 22.0 %all-to-all-done.2 = bf16[2,768,192]{2,0,1:T(2,128)(2,1)S(1)} async-done(((bf16[2,768,192]{2,0,1:T(2,128)(2,1)}), bf16[2,768,192]{2,0,1:T(2,128)(2,1)S(1)}, u32[]{:S(2)}, u32[]{:S(2)}) %all-to-all-start.2) | async-done | bytes 589856 | tf_op jit(solution)/shard_map/all_to_all | solution.py:41
  174.4 1.1 fusion.11
  175.6 1.1 fusion.13
  178.2 2.2 convert_reduce_fusion
  181.2 1.1 convolution_bitcast_fusion
  183.1 1.8 copy-done
  184.8 1.1 copy.69
  186.0 33.2 %all_to_all.90 = bf16[128,12,192]{2,1,0:T(8,128)(2,1)S(1)} all-to-all(bf16[128,12,192]{2,1,0:T(8,128)(2,1)S(1)} %copy.69), channel_id=1, replica_groups=mesh['row'=64,'col'=4] {'row'}, dimensions={0} | all-to-all | bytes 1179648 | tf_op jit(solution)/shard_map/all_to_all | solution.py:21
  219.8 1.7 copy.72
  221.6 1.1 copy.73
  222.7 33.2 %all_to_all.91 = bf16[128,12,192]{2,1,0:T(8,128)(2,1)S(1)} all-to-all(bf16[128,12,192]{2,1,0:T(8,128)(2,1)S(1)} %copy.73), channel_id=1, replica_groups=mesh['row'=64,'col'=4] {'row'}, dimensions={0} | all-to-all | bytes 1179648 | tf_op jit(solution)/shard_map/all_to_all | solution.py:22
  257.6 2.6 convolution_convert_fusion
  260.2 1.8 copy.77
  262.0 10.0 %all-to-all-start.5 = ((bf16[2,768,192]{2,0,1:T(2,128)(2,1)}), bf16[2,768,192]{2,0,1:T(2,128)(2,1)S(1)}, u32[]{:S(2)}, u32[]{:S(2)}) async-start(bf16[2,768,192]{2,0,1:T(2,128)(2,1)} %copy.77), calls=%async_computation.6 | async-start | bytes 1572864 | tf_op jit(solution)/shard_map/all_to_all | solution.py:41
  272.2 22.5 %all-to-all-done.5 = bf16[2,768,192]{2,0,1:T(2,128)(2,1)S(1)} async-done(((bf16[2,768,192]{2,0,1:T(2,128)(2,1)}), bf16[2,768,192]{2,0,1:T(2,128)(2,1)S(1)}, u32[]{:S(2)}, u32[]{:S(2)}) %all-to-all-start.5) | async-done | bytes 589856 | tf_op jit(solution)/shard_map/all_to_all | solution.py:41
  295.5 1.1 fusion.4
  296.6 1.1 fusion.6
  299.2 2.6 fusion.23
  (45 shorter events, 13.3 us)
Async XLA Ops:
  6.5 5.7 %copy-start.2 = (bf16[12,192,128]{2,1,0:T(8,128)(2,1)S(1)}, bf16[12,192,128]{2,1,0:T(8,128)(2,1)}, u32[]{:S(2)}) copy-start(bf16[12,192,128]{2,1,0:T(8,128)(2,1)} %param.6) | copy-start | bytes 1769476
  6.5 5.7 %copy-start.3 = (bf16[2,5,128,128]{3,2,1,0:T(8,128)(2,1)S(1)}, bf16[2,5,128,128]{3,2,1,0:T(8,128)(2,1)}, u32[]{:S(2)}) copy-start(bf16[2,5,128,128]{3,2,1,0:T(8,128)(2,1)} %param.9) | copy-start | bytes 983044
  13.4 2.5 copy-start.1
  17.8 40.2 %all-to-all-start = ((bf16[128,12,192]{2,1,0:T(8,128)(2,1)}), bf16[128,12,192]{2,1,0:T(8,128)(2,1)S(1)}, u32[]{:S(2)}, u32[]{:S(2)}) async-start(bf16[128,12,192]{2,1,0:T(8,128)(2,1)} %copy.53), calls=%async_computation | async-start | bytes 2097152 | tf_op jit(solution)/shard_map/all_to_all | solution.py:22
  58.1 33.8 %all-to-all-start.1 = ((bf16[128,12,192]{2,1,0:T(8,128)(2,1)}), bf16[128,12,192]{2,1,0:T(8,128)(2,1)S(1)}, u32[]{:S(2)}, u32[]{:S(2)}) async-start(bf16[128,12,192]{2,1,0:T(8,128)(2,1)} %copy.58), calls=%async_computation.1 | async-start | bytes 2097152 | tf_op jit(solution)/shard_map/all_to_all | solution.py:21
  65.3 72.4 %reduce-scatter.2.cloned.1.call-start = ((), (), s32[]{:S(2)}) async-start(), calls=%async_computation.7 | async-start | bytes 2949120 | tf_op jit(solution)/shard_map/reduce_scatter | solution.py:25
  137.8 13.7 %copy-start.5 = (f32[2,128]{1,0:T(2,128)S(1)}, f32[2,128]{1,0:T(2,128)}, u32[]{:S(2)}) copy-start(f32[2,128]{1,0:T(2,128)} %param.10) | copy-start | bytes 3076
  140.7 32.9 %all-to-all-start.2 = ((bf16[2,768,192]{2,0,1:T(2,128)(2,1)}), bf16[2,768,192]{2,0,1:T(2,128)(2,1)S(1)}, u32[]{:S(2)}, u32[]{:S(2)}) async-start(bf16[2,768,192]{2,0,1:T(2,128)(2,1)} %copy.63), calls=%async_computation.3 | async-start | bytes 1572864 | tf_op jit(solution)/shard_map/all_to_all | solution.py:41
  151.2 106.4 %all-gather.2.cloned.1.call-start = ((), (), s32[]{:S(2)}) async-start(), calls=%async_computation.8 | async-start | bytes 2949120 | tf_op jit(solution)/shard_map/all_gather | solution.py:37
  177.3 0.8 copy-start.6
  178.2 3.0 copy-start.4
  182.3 2.5 copy-start
  262.0 32.7 %all-to-all-start.5 = ((bf16[2,768,192]{2,0,1:T(2,128)(2,1)}), bf16[2,768,192]{2,0,1:T(2,128)(2,1)S(1)}, u32[]{:S(2)}, u32[]{:S(2)}) async-start(bf16[2,768,192]{2,0,1:T(2,128)(2,1)} %copy.77), calls=%async_computation.6 | async-start | bytes 1572864 | tf_op jit(solution)/shard_map/all_to_all | solution.py:41
Sparse Core Ops, SparseCore 0:
  94.8 42.8 reduce-scatter.1
  221.7 35.8 all-gather.1
where the time goes:
time: 310 us; the launch traced here: 309 us
  waiting for transfers between devices  140 us (45%)
  blocking collectives  66.5 us (21%)
  starting transfers between devices  40.7 us (13%)
  local copies, waits for them, and re-layouts  22.5 us (7%)
  between operations  13.7 us (4%)
  other arithmetic  13.2 us (4%)
  matrix products  11.9 us (4%)
    all_to_all x2, waiting for transfers between devices, one_update(): lax.all_to_all(product, 'row', split_axis=1, concat_axis=0, tiled=True)  44.6 us
    reduce_scatter x1, waiting for transfers between devices, one_update(): lax.psum_scatter(jnp.einsum('cik,cjk->jci', left_side, right_side, prefer...  43 us
    all_to_all x1, blocking collectives, one_update(): lax.all_to_all(right_side, 'row', split_axis=0, concat_axis=1, tiled=True)  33.2 us
    all_to_all x1, blocking collectives, one_update(): lax.all_to_all(left_side, 'row', split_axis=0, concat_axis=1, tiled=True)  33.2 us
    all_to_all x1, waiting for transfers between devices, one_update(): lax.all_to_all(left_side, 'row', split_axis=0, concat_axis=1, tiled=True)  25.9 us
    all_to_all x1, waiting for transfers between devices, one_update(): lax.all_to_all(right_side, 'row', split_axis=0, concat_axis=1, tiled=True)  25.6 us
    all_to_all x2, starting transfers between devices, one_update(): lax.all_to_all(product, 'row', split_axis=1, concat_axis=0, tiled=True)  20.5 us
    all_to_all x1, starting transfers between devices, one_update(): lax.all_to_all(right_side, 'row', split_axis=0, concat_axis=1, tiled=True)  12.7 us
  transfers between devices with their start and end apart: 6, of which 6 were waited for; matrix products, arithmetic and copies ran while one was open for 1% of the time, Pallas kernels for 0%

commit v1 on v0

v1 whole, which is shorter than its diff:
```python
import functools

import jax
import jax.numpy as jnp
from jax import lax
from jax.experimental import pallas as pl
from jax.experimental.pallas import tpu as pltpu
from jax.sharding import PartitionSpec as P

MESH = pl.DeviceIdType.MESH
F32 = jnp.float32
BF16 = jnp.bfloat16
ROWS = 64
CH = 128
IL = 6
CHUNKS = 4
CW = CH // CHUNKS
NT = (((1,), (1,)), ((), ()))
NN = (((1,), (0,)), ((), ()))
TN = (((0,), (0,)), ((), ()))


def dot(a, b, dims):
    return lax.dot_general(a, b, dims, preferred_element_type=F32)


def kernel(
    pair_ref, mask_s, mask_v, in_gain, w_in, out_gain, w_out, out_ref,
    zin, zbuf, xn, gate, wt, bf, b, lr0, lr1, rc, lt, sel, selt, xs, xp, ts, tri, tf, gcol, pm,
    x_send, x_recv, lr_send, lr_recv, t_send, t_recv,
):
    r = lax.axis_index("row")
    q = lax.axis_index("col")
    xhi = q // 2
    c = q % 2
    partner = (r, xhi * 2 + 1 - c)
    z_me = r // 8
    chip = r * 2 + xhi

    lr0[...] = jnp.zeros_like(lr0)
    lr1[...] = jnp.zeros_like(lr1)

    barrier = pltpu.get_barrier_semaphore()

    @pl.loop(1, 256)
    def _(s):
        t = (r * 4 + q + s) % 256
        pl.semaphore_signal(barrier, inc=1, device_id=(t // 4, t % 4), device_id_type=MESH)

    for u in range(2):
        for v in range(4):
            turned = w_in[u, v].astype(F32).T.astype(BF16)
            for g in range(CHUNKS):
                wt[u, g, v * CW : (v + 1) * CW, :] = turned[g * CW : (g + 1) * CW]
        gcol[u] = jnp.broadcast_to(out_gain[u : u + 1, :], (CH, CH)).T
    row_id = lax.broadcasted_iota(jnp.int32, (512, 384), 0)
    col_id = lax.broadcasted_iota(jnp.int32, (512, 384), 1)
    hit = (row_id % 8 < IL) & ((row_id // 8) * IL + row_id % 8 == col_id)
    sel[...] = jnp.where(hit, 1.0, 0.0).astype(BF16)
    row_id = lax.broadcasted_iota(jnp.int32, (384, 512), 1)
    col_id = lax.broadcasted_iota(jnp.int32, (384, 512), 0)
    hit = (row_id % 8 < IL) & ((row_id // 8) * IL + row_id % 8 == col_id)
    selt[...] = jnp.where(hit, 1.0, 0.0).astype(BF16)
    for k in range(3):
        cols = mask_v[pl.ds(xhi * 3 + k, 1), :].astype(F32)
        for i in range(IL):
            pm[i : i + 1, k * 128 : (k + 1) * 128] = cols * mask_s[r * 12 + c * IL + i].astype(F32)

    pl.semaphore_wait(barrier, 255)

    swap = pltpu.make_async_remote_copy(
        pair_ref.at[pl.ds((1 - c) * IL, IL)], zin.at[...], x_send.at[0], x_recv.at[0],
        device_id=partner, device_id_type=MESH,
    )
    swap.start()
    zbuf[:, pl.ds(pl.multiple_of(c * 192, 64), 192), :] = pair_ref[pl.ds(c * IL, IL)]
    swap.wait()
    zbuf[:, pl.ds(pl.multiple_of((1 - c) * 192, 64), 192), :] = zin[...]

    for u in range(2):
        lr = (lr0, lr1)[u]

        @pl.loop(0, IL)
        def _(i):
            val = zbuf[i].astype(F32)
            shifted = val - jnp.mean(val, axis=-1, keepdims=True)
            spread = jnp.mean(shifted * shifted, axis=-1, keepdims=True)
            xn[i] = (shifted * lax.rsqrt(spread + 1e-05) * in_gain[u : u + 1, :]).astype(BF16)

        if u == 0:
            core_to, slot = xhi, lambda: lr0.at[:, :, r * 2 + c, pl.ds(0, IL), :]
            is_self = xhi == c
        else:
            core_to, slot = c, lambda: lr1.at[:, pl.ds(xhi * 3, 3), r, pl.ds(0, IL), :]
            is_self = c == c

        @pl.loop(0, CHUNKS)
        def _(step):
            g = (z_me // 2 + 2 + step) % CHUNKS

            @pl.loop(0, IL)
            def _(i):
                o = dot(wt[u, g], xn[i], NT)
                mask = pm[pl.ds(i, 1), :]
                for s in range(2):
                    side = jax.nn.sigmoid(o[2 * s * CW : (2 * s + 1) * CW])
                    side = side * o[(2 * s + 1) * CW : (2 * s + 2) * CW] * mask
                    for k in range(3):
                        bf[s, k, pl.ds(i, CW, stride=8), :] = side[:, k * 128 : (k + 1) * 128]

            for s in range(2):
                for k in range(3):
                    b[pl.ds(g * CW, CW), s, k] = bf[s, k].reshape(CW, 8, 128).astype(BF16)

            @pl.loop(0, CW)
            def _(n):
                m = g * CW + (n + chip) % CW
                src = b.at[m, :, :, pl.ds(0, IL), :]
                mine = (m == chip) & is_self

                @pl.when(mine)
                def _():
                    pltpu.make_async_copy(src, slot(), lr_recv.at[u]).start()

                @pl.when(jnp.logical_not(mine))
                def _():
                    pltpu.make_async_remote_copy(
                        src, slot(), lr_send.at[u], lr_recv.at[u],
                        device_id=(m // 2, (m % 2) * 2 + core_to), device_id_type=MESH,
                    ).start()

        @pl.loop(0, IL)
        def _(i):
            gate[i] = jax.nn.sigmoid(dot(xn[i], w_in[u, 4], NN))

        whole = b.at[:, :, :, pl.ds(0, IL), :]
        most = b.at[pl.ds(0, CH - 1), :, :, pl.ds(0, IL), :]
        one = b.at[0, :, :, pl.ds(0, IL), :]
        pltpu.make_async_copy(whole, whole, lr_recv.at[u]).wait()
        pltpu.make_async_copy(most, most, lr_send.at[u]).wait()
        if u == 0:
            @pl.when(jnp.logical_not(is_self))
            def _():
                pltpu.make_async_copy(one, one, lr_send.at[u]).wait()

        if u == 0:
            for half in range(2):
                part = [lr0[1, k, 64 * half : 64 * half + 64].reshape(512, 128) for k in range(3)]
                rc[384 * half : 384 * half + 384, :] = dot(
                    selt[...], jnp.concatenate(part, axis=1), NN
                ).astype(BF16)

            def product(h, n):
                at = pl.ds(h * 64 + n * 16, 16)
                left = [lr0[0, k, at].reshape(128, 128) for k in range(3)]
                return dot(jnp.concatenate(left, axis=1), rc[...], NT)
        else:
            for half in range(2):
                part = [lr1[0, half * 3 + k].reshape(512, 128) for k in range(3)]
                lt[half] = dot(sel[...], jnp.concatenate(part, axis=1), NT).astype(BF16)

            def product(h, n):
                left = lt[h, pl.ds(pl.multiple_of(n * 128, 128), 128)]
                right = [lr1[1, k].reshape(512, 128) for k in range(6)]
                return dot(left, jnp.concatenate(right, axis=1), NN)

        @pl.loop(0, 4)
        def _(n):
            xs[u, pl.ds(pl.multiple_of(n * 128, 128), 128), :] = product(1 - c, n).astype(BF16)

        give = pltpu.make_async_remote_copy(
            xs.at[u], xp.at[u], x_send.at[1 + u], x_recv.at[1 + u],
            device_id=partner, device_id_type=MESH,
        )
        give.start()
        give.wait()

        here = r // 32 == c

        @pl.loop(0, 4)
        def _(step):
            n = (z_me + 2 + step) % 4
            p = product(c, n) + xp[u, pl.ds(pl.multiple_of(n * 128, 128), 128), :].astype(F32)
            for h in range(2):
                for k in range(3):
                    tile = p[:, (h * 3 + k) * 128 : (h * 3 + k + 1) * 128]
                    ts[u, pl.ds(n * 16, 16), h, k] = tile.reshape(16, 8, 128).astype(BF16)

            @pl.loop(0, 32)
            def _(s):
                t = (s + chip * 2 + c) % 32
                e = n * 16 + t // 2
                h = t % 2
                to_r = c * 32 + e // 2
                to_q = h * 2 + e % 2
                src = ts.at[u, e, h, :, pl.ds(0, IL), :]
                dst = tri.at[u, :, chip, pl.ds(0, IL), :]
                mine = (to_r == r) & (to_q == q)

                @pl.when(mine)
                def _():
                    pltpu.make_async_copy(src, dst, t_recv.at[u]).start()

                @pl.when(jnp.logical_not(mine))
                def _():
                    pltpu.make_async_remote_copy(
                        src, dst, t_send.at[u], t_recv.at[u],
                        device_id=(to_r, to_q), device_id_type=MESH,
                    ).start()

        whole = tri.at[u, :, :, pl.ds(0, IL), :]
        most = tri.at[u, :, pl.ds(0, CH - 1), pl.ds(0, IL), :]
        one = tri.at[u, :, 0, pl.ds(0, IL), :]
        pltpu.make_async_copy(whole, whole, t_recv.at[u]).wait()

        @pl.loop(0, 3)
        def _(k):
            tf[...] = tri[u, k].astype(F32).reshape(CH * 8, 128)
            at = pl.ds(pl.multiple_of(k * 128, 128), 128)
            for i in range(IL):
                val = tf[pl.ds(i, CH, stride=8), :]
                shifted = val - jnp.mean(val, axis=0, keepdims=True)
                spread = jnp.mean(shifted * shifted, axis=0, keepdims=True)
                normed = (shifted * lax.rsqrt(spread + 1e-05) * gcol[u]).astype(BF16)
                term = dot(normed, w_out[u], TN) * gate[i, at, :]
                zbuf[i, at, :] = (zbuf[i, at, :].astype(F32) + term).astype(BF16)

        pltpu.make_async_copy(most, most, t_send.at[u]).wait()

        @pl.when(jnp.logical_not(here))
        def _():
            pltpu.make_async_copy(one, one, t_send.at[u]).wait()

    back = pltpu.make_async_remote_copy(
        zbuf.at[:, pl.ds(pl.multiple_of((1 - c) * 192, 64), 192), :], out_ref.at[pl.ds(c * IL, IL)],
        x_send.at[3], x_recv.at[3], device_id=partner, device_id_type=MESH,
    )
    back.start()
    out_ref[pl.ds(c * IL, IL)] = zbuf[:, pl.ds(pl.multiple_of(c * 192, 64), 192), :]
    back.wait()


def on_device(pair, residue_mask, in_gain, w_in, out_gain, w_out):
    vmem = pl.BlockSpec(memory_space=pltpu.VMEM)
    smem = pl.BlockSpec(memory_space=pltpu.SMEM)
    dma = pltpu.SemaphoreType.DMA
    return pl.pallas_call(
        kernel,
        out_shape=jax.ShapeDtypeStruct(pair.shape, BF16),
        in_specs=[vmem, smem, vmem, vmem, vmem, vmem, vmem],
        out_specs=vmem,
        scratch_shapes=[
            pltpu.VMEM((IL, 192, CH), BF16),
            pltpu.VMEM((IL, 384, CH), BF16),
            pltpu.VMEM((IL, 384, CH), BF16),
            pltpu.VMEM((IL, 384, CH), F32),
            pltpu.VMEM((2, CHUNKS, 4 * CW, CH), BF16),
            pltpu.VMEM((2, 3, CW * 8, 128), F32),
            pltpu.VMEM((CH, 2, 3, 8, 128), BF16),
            pltpu.VMEM((2, 3, 128, 8, 128), BF16),
            pltpu.VMEM((2, 6, 64, 8, 128), BF16),
            pltpu.VMEM((768, 384), BF16),
            pltpu.VMEM((2, 512, 512), BF16),
            pltpu.VMEM((512, 384), BF16),
            pltpu.VMEM((384, 512), BF16),
            pltpu.VMEM((2, 512, 768), BF16),
            pltpu.VMEM((2, 512, 768), BF16),
            pltpu.VMEM((2, 64, 2, 3, 8, 128), BF16),
            pltpu.VMEM((2, 3, CH, 8, 128), BF16),
            pltpu.VMEM((CH * 8, 128), F32),
            pltpu.VMEM((2, CH, 128), F32),
            pltpu.VMEM((8, 384), F32),
            dma((4,)), dma((4,)), dma((2,)), dma((2,)), dma((2,)), dma((2,)),
        ],
        compiler_params=pltpu.CompilerParams(
            collective_id=0, has_side_effects=True, vmem_limit_bytes=48 * 2**20
        ),
        name="triangle",
    )(pair, residue_mask, residue_mask.reshape(6, 128), in_gain, w_in, out_gain, w_out)


def solution(mesh):
    placed = (P("row", "col", None), P(), P(), P(), P(), P())
    return jax.shard_map(
        on_device, mesh=mesh, in_specs=placed, out_specs=P("row", "col", None), check_vma=False
    )
```

time: 310 us -> 138 us (0.45)
  waiting for transfers between devices: 140 us -> 0 us
  Pallas kernels: 0 us -> 131 us
  blocking collectives: 66.5 us -> 0 us
  starting transfers between devices: 40.7 us -> 0 us
  local copies, waits for them, and re-layouts: 22.5 us -> 5.74 us
  between operations: 13.7 us -> 0.02 us
  other arithmetic: 13.2 us -> 0 us
  matrix products: 11.9 us -> 0 us
    pallas_call x0 -> x1, Pallas kernels: none -> 131 us  [on_device(): pl.pallas_call(kernel, out_shape=jax.ShapeDtypeStruct(pair.shape, BF16),...]
    all_to_all x4 -> x0, waiting for transfers between devices: 96 us -> none  [the longest x2 44.6 us: one_update(): lax.all_to_all(product, 'row', split_axis=1, concat_axis=0, tiled=True)]
    all_to_all x2 -> x0, blocking collectives: 66.5 us -> none  [the longest x1 33.2 us: one_update(): lax.all_to_all(right_side, 'row', split_axis=0, concat_axis=1, tiled=True)]
    reduce_scatter x1 -> x0, waiting for transfers between devices: 43 us -> none  [one_update(): lax.psum_scatter(jnp.einsum('cik,cjk->jci', left_side, right_side, prefer...]
    all_to_all x4 -> x0, starting transfers between devices: 40.5 us -> none  [the longest x2 20.5 us: one_update(): lax.all_to_all(product, 'row', split_axis=1, concat_axis=0, tiled=True)]
    dot_general x6 -> x0, matrix products: 11.9 us -> none  [the longest x2 4.78 us: one_update(): jnp.einsum('crj,cd->drj', tri_normed, weight_out, preferred_element_type=...]
    convert_element_type x9 -> x0, local copies, waits for them, and re-layouts: 10.7 us -> none  [the longest x2 3.08 us: one_update(): (jax.nn.sigmoid(projected[2]) * projected[3] * pair_mask).astype(jnp.bflo...]
    reduce_sum x7 -> x0, other arithmetic: 7.83 us -> none  [the longest x4 5 us: layer_norm(): spread = jnp.mean(shifted * shifted, axis=axis_index, keepdims=True)]
  transfers between devices with their start and end apart: 6 -> 0, of which waited for: 6 -> 0; matrix products, arithmetic and copies ran while one was open for 1% -> 0% of each run, Pallas kernels for 0% -> 0%
where the time goes in v1:
time: 138 us; the launch traced here: 137 us
  Pallas kernels  131 us (95%)
  local copies, waits for them, and re-layouts  5.74 us (4%)
    pallas_call x1, Pallas kernels, on_device(): pl.pallas_call(kernel, out_shape=jax.ShapeDtypeStruct(pair.shape, BF16),...  131 us
    unnamed x13, local copies, waits for them, and re-layouts  5.74 us

profile of v1, /device:TPU:32, one launch (start us, length us, event | category | flops | bytes accessed | tf_op | source)
XLA Modules:
  0.0 137.0 jit_solution(16637510571000979288)
XLA Ops:
  0.0 0.0 copy-start.4
  0.0 0.7 copy-done.4
  0.7 0.0 copy-start
  0.7 1.1 copy-done
  1.7 0.0 copy-start.1
  1.7 1.0 copy-done.1
  2.7 0.0 copy-start.2
  2.7 0.8 copy-done.2
  3.6 0.0 copy-start.3
  3.6 0.7 copy-done.3
  4.2 0.0 copy-start.5
  4.2 0.7 copy-done.5
  4.9 131.2 %triangle.1 = bf16[12,192,128]{2,1,0:T(8,128)(2,1)S(1)} custom-call(bf16[12,192,128]{2,1,0:T(8,128)(2,1)S(1)} %copy-done, s32[768]{0:T(1024)S(1)} %copy-done.3, s32[6,128]{1,0:T(8,128)S(1)} %bitcast.1, f32[2,128]{1,0:T(2,128)S(1)} %copy-done.4, bf16[2,5,128,128]{3,2,1,0:T(8,128)(2,1)S(1)} %copy-done.1, f32[2,128]{1,0:T(2,128)S(1)} %copy-done.5, ...), custom_call_target="tpu_custom_call" | custom-call | tf_op jit(solution)/shard_map/triangle/pallas_call | solution.py:247
  136.2 0.8 copy.8
Async XLA Ops:
  0.0 0.7 copy-start.4
  0.7 1.1 copy-start
  1.7 1.0 copy-start.1
  2.7 0.8 copy-start.2
  3.6 0.7 copy-start.3
  4.2 0.7 copy-start.5

commit v2 on v0

v2 whole, which is shorter than its diff:
```python
import jax
import jax.numpy as jnp
from jax import lax
from jax.experimental import pallas as pl
from jax.experimental.pallas import tpu as pltpu
from jax.sharding import PartitionSpec as P

MESH = pl.DeviceIdType.MESH
F32 = jnp.float32
BF16 = jnp.bfloat16
CH = 128
IL = 6
CHUNKS = 4
CW = CH // CHUNKS
NT = (((1,), (1,)), ((), ()))
NN = (((1,), (0,)), ((), ()))
TN = (((0,), (0,)), ((), ()))


def dot(a, b, dims):
    return lax.dot_general(a, b, dims, preferred_element_type=F32)


def sigmoid(v):
    return 0.5 * jnp.tanh(0.5 * v) + 0.5


def halves(a, b):
    return jnp.concatenate([a, b], axis=1)


def kernel(
    pair_hbm, mask_hbm, mask6_hbm, in_gain_hbm, w_in_hbm, out_gain_hbm, w_out_hbm, out_ref,
    pair, mask_s, mask_v, in_gain, w_in, out_gain, w_out,
    zin, zbuf, zown, xn, gate, wt, bf, b, lr0, lr1, rc, lt, tl, sel, selt, xs0, xp0, xs1, xp1,
    ts, tri, tf, gcol, pm, ones,
    in_sem, x_send, x_recv, p_send, p_recv, lr_send, lr_recv, t_send, t_recv,
):
    r = lax.axis_index("row")
    q = lax.axis_index("col")
    xhi = q // 2
    c = q % 2
    partner = (r, xhi * 2 + 1 - c)
    chip = r * 2 + xhi
    main_at = pl.ds(pl.multiple_of(c * 64, 64), 128)
    tail_at = pl.ds(pl.multiple_of((1 - c) * 128, 128), 64)
    mine_at = pl.ds(pl.multiple_of(c * 192, 64), 192)
    other_at = pl.ds(pl.multiple_of((1 - c) * 192, 64), 192)
    six = pl.ds(0, IL)

    loads = [
        pltpu.make_async_copy(src, dst, in_sem.at[n])
        for n, (src, dst) in enumerate(
            (
                (pair_hbm, pair), (mask_hbm, mask_s), (mask6_hbm, mask_v), (in_gain_hbm, in_gain),
                (w_in_hbm, w_in), (out_gain_hbm, out_gain), (w_out_hbm, w_out),
            )
        )
    ]
    for load in loads:
        load.start()

    lr0[1] = jnp.zeros(lr0.shape[1:], BF16)
    lr1[...] = jnp.zeros_like(lr1)

    bits = [r // 2**k % 2 for k in range(4)]

    def chunk_of(step):
        zh = r // 16
        b1, b0 = 1 - step // 2, 1 - step % 2
        return 2 * ((zh // 2 + b1) % 2) + (zh % 2 + b0) % 2

    def chips(g, last, visit):
        @pl.loop(0, 4)
        def _(hi):
            b3, b2 = 1 - hi // 2, 1 - hi % 2
            base = g * 16 + 8 * ((bits[3] + b3) % 2) + 4 * ((bits[2] + b2) % 2)
            for low in range(7, -1, -1):
                e = base
                for k in range(2):
                    e = e + 2**k * (1 - bits[k] if low >> (k + 1) & 1 else bits[k])
                h = 1 - xhi if low & 1 else xhi
                visit(e, h, low == 0 and last & (hi == 3))

    barrier = pltpu.get_barrier_semaphore()
    pl.semaphore_signal(barrier, inc=1, device_id=partner, device_id_type=MESH)

    @pl.loop(0, CHUNKS)
    def _(step):
        def greet(e, h, mine):
            def signal():
                pl.semaphore_signal(barrier, inc=1, device_id=(e, h * 2 + c), device_id_type=MESH)

            if mine is False:
                signal()
            else:
                pl.when(jnp.logical_not(mine))(signal)

        chips(chunk_of(step), step == 3, greet)

    for load in loads:
        load.wait()

    def turn(u):
        for v in range(4):
            turned = w_in[u, v].astype(F32).T.astype(BF16)
            for g in range(CHUNKS):
                wt[u, g, v * CW : (v + 1) * CW, :] = turned[g * CW : (g + 1) * CW]
        gcol[u] = jnp.broadcast_to(out_gain[u : u + 1, :], (CH, CH)).T

    def norm(u):
        @pl.loop(0, IL)
        def _(i):
            val = zbuf[i]
            shifted = val.astype(F32) - dot(val, ones[...], NN) * (1.0 / CH)
            spread = dot((shifted * shifted).astype(BF16), ones[...], NN) * (1.0 / CH)
            xn[i] = (shifted * lax.rsqrt(spread + 1e-05) * in_gain[u : u + 1, :]).astype(BF16)

    def gates(u):
        @pl.loop(0, IL)
        def _(i):
            gate[i] = sigmoid(dot(xn[i], w_in[u, 4], NN))

    def to_own(src):
        @pl.loop(0, IL)
        def _(i):
            zbuf[i, 0:128] = src[i, main_at]
            zbuf[i, 128:256] = src[IL + i, main_at]
            zbuf[i, 256:320] = src[i, tail_at]
            zbuf[i, 320:384] = src[IL + i, tail_at]

    def project(u, g):
        @pl.loop(0, IL)
        def _(i):
            o = dot(wt[u, g], xn[i], NT)
            mask = pm[u, pl.ds(i, 1), :]
            for s in range(2):
                side = sigmoid(o[2 * s * CW : (2 * s + 1) * CW])
                side = side * o[(2 * s + 1) * CW : (2 * s + 2) * CW] * mask
                for k in range(3):
                    bf[s, k, pl.ds(i, CW, stride=8), :] = side[:, k * 128 : (k + 1) * 128]

        for s in range(2):
            for k in range(3):
                b[pl.ds(g * CW, CW), s, k] = bf[s, k].reshape(CW, 8, 128).astype(BF16)

    def send(src, dst, send_sem, recv_sem, to, mine):
        def remote():
            pltpu.make_async_remote_copy(
                src, dst, send_sem, recv_sem, device_id=to, device_id_type=MESH
            ).start()

        if mine is False:
            remote()
        else:
            pl.when(jnp.logical_not(mine))(remote)

            @pl.when(mine)
            def _():
                pltpu.make_async_copy(src, dst, recv_sem).start()

    lane = lax.broadcasted_iota(jnp.int32, (1, 128), 1)
    row_mask = [mask_s[r * 12 + i].astype(F32) for i in range(2 * IL)]
    main = mask_v[pl.ds(xhi * 3 + 2 * c, 1), :].astype(F32)
    tile = mask_v[pl.ds(xhi * 3 + 1, 1), :].astype(F32)
    swapped = halves(tile[:, 64:], tile[:, :64])
    tail = jnp.where((lane < 64) == (c == 0), tile, swapped)
    for i in range(IL):
        pm[0, i : i + 1, 0:128] = main * row_mask[i]
        pm[0, i : i + 1, 128:256] = main * row_mask[IL + i]
        pm[0, i : i + 1, 256:384] = tail * jnp.where(lane < 64, row_mask[i], row_mask[IL + i])
        for k in range(3):
            cols = mask_v[pl.ds(xhi * 3 + k, 1), :].astype(F32)
            pm[1, i : i + 1, k * 128 : (k + 1) * 128] = cols * jnp.where(
                c == 0, row_mask[i], row_mask[IL + i]
            )

    ones[...] = jnp.ones_like(ones)
    turn(0)
    to_own(pair)
    norm(0)
    project(0, chunk_of(0))

    pl.semaphore_wait(barrier, 128)

    for u in range(2):
        @pl.loop(0, CHUNKS)
        def _(step):
            g = chunk_of(step)
            if u == 0:
                @pl.when(step > 0)
                def _():
                    project(u, g)
            else:
                project(u, g)

            def post(e, h, mine):
                if u == 0:
                    slot = lr0.at[:, :, xhi, r, six, :]
                else:
                    slot = lr1.at[:, pl.ds(xhi * 3, 3), r, six, :]
                send(
                    b.at[e * 2 + h, :, :, six, :], slot,
                    lr_send.at[u], lr_recv.at[u], (e, h * 2 + c), mine,
                )

            chips(g, step == 3, post)

        if u == 0:
            swap = pltpu.make_async_remote_copy(
                pair.at[pl.ds((1 - c) * IL, IL)], zin.at[...], x_send.at[0], x_recv.at[0],
                device_id=partner, device_id_type=MESH,
            )
            swap.start()
            turn(1)
            k_id = lax.broadcasted_iota(jnp.int32, (512, 384), 0)
            i_id = lax.broadcasted_iota(jnp.int32, (512, 384), 1)
            row = k_id % 256 // 8 * 12 + k_id // 256 * IL + k_id % 8
            sel[...] = jnp.where((k_id % 8 < IL) & (row == i_id), 1.0, 0.0).astype(BF16)
            k_id = lax.broadcasted_iota(jnp.int32, (384, 512), 1)
            i_id = lax.broadcasted_iota(jnp.int32, (384, 512), 0)
            row = k_id % 256 // 8 * 12 + k_id // 256 * IL + k_id % 8
            selt[...] = jnp.where((k_id % 8 < IL) & (row == i_id), 1.0, 0.0).astype(BF16)
            swap.wait()
            zbuf[:, mine_at, :] = pair[pl.ds(c * IL, IL)]
            zbuf[:, other_at, :] = zin[...]
        else:
            swap = pltpu.make_async_remote_copy(
                zbuf.at[:, other_at, :], zown.at[pl.ds(c * IL, IL)], x_send.at[1], x_recv.at[1],
                device_id=partner, device_id_type=MESH,
            )
            swap.start()
            zown[pl.ds(c * IL, IL)] = zbuf[:, mine_at, :]
            swap.wait()
            to_own(zown)
        norm(u)
        gates(u)

        whole = b.at[:, :, :, six, :]
        most = b.at[pl.ds(0, CH - 1), :, :, six, :]
        pltpu.make_async_copy(whole, whole, lr_recv.at[u]).wait()
        pltpu.make_async_copy(most, most, lr_send.at[u]).wait()

        if u == 0:
            xs, xp = xs0, xp0
            for s in range(2):
                t0, t1 = lr0[s, 2, 0].reshape(512, 128), lr0[s, 2, 1].reshape(512, 128)
                tl[s, 0] = halves(t0[:, :64], t1[:, :64])
                tl[s, 1] = halves(t0[:, 64:], t1[:, 64:])
            for half in range(2):
                at = slice(half * 32, half * 32 + 32)
                parts = [
                    jnp.concatenate(
                        [lr0[1, d, 0, at].reshape(256, 128), lr0[1, d, 1, at].reshape(256, 128),
                         tl[1, d, half * 256 : half * 256 + 256]], axis=1,
                    )
                    for d in range(2)
                ]
                rc[384 * half : 384 * half + 384, :] = dot(
                    selt[...], jnp.concatenate(parts, axis=0), NN
                ).astype(BF16)

            def product(d, n):
                at = pl.ds(n * 16, 16)
                left = [lr0[0, d, h, at].reshape(128, 128) for h in range(2)]
                left.append(tl[0, d, pl.ds(pl.multiple_of(n * 128, 128), 128), :])
                return dot(jnp.concatenate(left, axis=1), rc[...], NT)
        else:
            xs, xp = xs1, xp1
            for half in range(2):
                part = [lr1[0, half * 3 + k].reshape(512, 128) for k in range(3)]
                turned = dot(sel[...], jnp.concatenate(part, axis=1), NT).astype(BF16)
                for d in range(2):
                    lt[d, half * 256 : half * 256 + 256] = turned[d * 256 : d * 256 + 256]
            t0, t1 = lr1[1, 1].reshape(512, 128), lr1[1, 4].reshape(512, 128)
            tl[0, 0] = halves(t0[:, :64], t1[:, :64])
            tl[0, 1] = halves(t0[:, 64:], t1[:, 64:])

            def product(d, n):
                at = pl.ds(pl.multiple_of(n * 128, 128), 128)
                left = jnp.concatenate([lt[0, at], lt[1, at]], axis=0)
                right = [lr1[1, h * 3 + 2 * d].reshape(512, 128) for h in range(2)]
                return dot(left, jnp.concatenate(right + [tl[0, d]], axis=1), NN)

        def give(n):
            return pltpu.make_async_remote_copy(
                xs.at[n], xp.at[n], p_send.at[u, n], p_recv.at[u, n],
                device_id=partner, device_id_type=MESH,
            )

        @pl.loop(0, CHUNKS)
        def _(step):
            n = chunk_of(step)
            xs[n] = product(1 - c, n).astype(BF16)
            give(n).start()

        @pl.loop(0, CHUNKS)
        def _(step):
            n = chunk_of(step)
            p = product(c, n)
            give(n).wait_recv()
            p = p + xp[n].astype(F32)
            at = pl.ds(n * 16, 16)
            if u == 0:
                for h in range(2):
                    for k in range(3):
                        tile = p[:, (h * 3 + k) * 128 : (h * 3 + k + 1) * 128]
                        ts[at, h, k] = tile.reshape(16, 8, 128).astype(BF16)
            else:
                low, high = p[0:128], p[128:256]
                for h in range(2):
                    cols = slice(256 + h * 64, 320 + h * 64)
                    ts[at, h, 0] = low[:, h * 128 : h * 128 + 128].reshape(16, 8, 128).astype(BF16)
                    ts[at, h, 1] = high[:, h * 128 : h * 128 + 128].reshape(16, 8, 128).astype(BF16)
                    tile = halves(low[:, cols], high[:, cols])
                    ts[at, h, 2] = tile.reshape(16, 8, 128).astype(BF16)

            def post(e, h, mine):
                send(
                    ts.at[e, h, :, six, :], tri.at[u, :, chip, six, :],
                    t_send.at[u], t_recv.at[u], (e, h * 2 + c), mine,
                )

            chips(n, step == 3, post)

        for n in range(CHUNKS):
            give(n).wait_send()
        whole = tri.at[u, :, :, six, :]
        most = tri.at[u, :, pl.ds(0, CH - 1), six, :]
        pltpu.make_async_copy(whole, whole, t_recv.at[u]).wait()

        @pl.loop(0, 3)
        def _(k):
            tf[...] = tri[u, k].astype(F32).reshape(CH * 8, 128)
            at = pl.ds(pl.multiple_of(k * 128, 128), 128)
            for i in range(IL):
                val = tf[pl.ds(i, CH, stride=8), :]
                shifted = val - jnp.mean(val, axis=0, keepdims=True)
                spread = jnp.mean(shifted * shifted, axis=0, keepdims=True)
                normed = (shifted * lax.rsqrt(spread + 1e-05) * gcol[u]).astype(BF16)
                term = dot(normed, w_out[u], TN) * gate[i, at, :]
                zbuf[i, at, :] = (zbuf[i, at, :].astype(F32) + term).astype(BF16)

        pltpu.make_async_copy(most, most, t_send.at[u]).wait()
        if u == 0:
            norm(1)

    @pl.loop(0, IL)
    def _(i):
        out_ref[i, main_at] = zbuf[i, 0:128]
        out_ref[IL + i, main_at] = zbuf[i, 128:256]
        out_ref[i, tail_at] = zbuf[i, 256:320]
        out_ref[IL + i, tail_at] = zbuf[i, 320:384]


def on_device(pair, residue_mask, in_gain, w_in, out_gain, w_out):
    hbm = pl.BlockSpec(memory_space=pl.ANY)
    dma = pltpu.SemaphoreType.DMA
    return pl.pallas_call(
        kernel,
        out_shape=jax.ShapeDtypeStruct(pair.shape, BF16),
        in_specs=[hbm] * 7,
        out_specs=pl.BlockSpec(memory_space=pltpu.VMEM),
        scratch_shapes=[
            pltpu.VMEM(pair.shape, BF16),
            pltpu.SMEM((768,), jnp.int32),
            pltpu.VMEM((6, 128), jnp.int32),
            pltpu.VMEM(in_gain.shape, F32),
            pltpu.VMEM(w_in.shape, BF16),
            pltpu.VMEM(out_gain.shape, F32),
            pltpu.VMEM(w_out.shape, BF16),
            pltpu.VMEM((IL, 192, CH), BF16),
            pltpu.VMEM((IL, 384, CH), BF16),
            pltpu.VMEM((2 * IL, 192, CH), BF16),
            pltpu.VMEM((IL, 384, CH), BF16),
            pltpu.VMEM((IL, 384, CH), F32),
            pltpu.VMEM((2, CHUNKS, 4 * CW, CH), BF16),
            pltpu.VMEM((2, 3, CW * 8, 128), F32),
            pltpu.VMEM((CH, 2, 3, 8, 128), BF16),
            pltpu.VMEM((2, 3, 2, 64, 8, 128), BF16),
            pltpu.VMEM((2, 6, 64, 8, 128), BF16),
            pltpu.VMEM((768, 384), BF16),
            pltpu.VMEM((2, 512, 512), BF16),
            pltpu.VMEM((2, 2, 512, 128), BF16),
            pltpu.VMEM((512, 384), BF16),
            pltpu.VMEM((384, 512), BF16),
            pltpu.VMEM((4, 128, 768), BF16),
            pltpu.VMEM((4, 128, 768), BF16),
            pltpu.VMEM((4, 256, 384), BF16),
            pltpu.VMEM((4, 256, 384), BF16),
            pltpu.VMEM((64, 2, 3, 8, 128), BF16),
            pltpu.VMEM((2, 3, CH, 8, 128), BF16),
            pltpu.VMEM((CH * 8, 128), F32),
            pltpu.VMEM((2, CH, 128), F32),
            pltpu.VMEM((2, 8, 384), F32),
            pltpu.VMEM((CH, 128), BF16),
            dma((7,)), dma((2,)), dma((2,)), dma((2, 4)), dma((2, 4)),
            dma((2,)), dma((2,)), dma((2,)), dma((2,)),
        ],
        compiler_params=pltpu.CompilerParams(
            collective_id=0, has_side_effects=True, vmem_limit_bytes=48 * 2**20
        ),
        name="triangle",
    )(pair, residue_mask, residue_mask.reshape(6, 128), in_gain, w_in, out_gain, w_out)


def solution(mesh):
    placed = (P("row", "col", None), P(), P(), P(), P(), P())
    return jax.shard_map(
        on_device, mesh=mesh, in_specs=placed, out_specs=P("row", "col", None), check_vma=False
    )
```

time: 310 us -> 125 us (0.40)
  waiting for transfers between devices: 140 us -> 0 us
  Pallas kernels: 0 us -> 119 us
  blocking collectives: 66.5 us -> 0 us
  starting transfers between devices: 40.7 us -> 0 us
  local copies, waits for them, and re-layouts: 22.5 us -> 5.74 us
  between operations: 13.7 us -> 0.02 us
  other arithmetic: 13.2 us -> 0 us
  matrix products: 11.9 us -> 0 us
    pallas_call x0 -> x1, Pallas kernels: none -> 119 us  [on_device(): pl.pallas_call(kernel, out_shape=jax.ShapeDtypeStruct(pair.shape, BF16),...]
    all_to_all x4 -> x0, waiting for transfers between devices: 96 us -> none  [the longest x2 44.6 us: one_update(): lax.all_to_all(product, 'row', split_axis=1, concat_axis=0, tiled=True)]
    all_to_all x2 -> x0, blocking collectives: 66.5 us -> none  [the longest x1 33.2 us: one_update(): lax.all_to_all(right_side, 'row', split_axis=0, concat_axis=1, tiled=True)]
    reduce_scatter x1 -> x0, waiting for transfers between devices: 43 us -> none  [one_update(): lax.psum_scatter(jnp.einsum('cik,cjk->jci', left_side, right_side, prefer...]
    all_to_all x4 -> x0, starting transfers between devices: 40.5 us -> none  [the longest x2 20.5 us: one_update(): lax.all_to_all(product, 'row', split_axis=1, concat_axis=0, tiled=True)]
    dot_general x6 -> x0, matrix products: 11.9 us -> none  [the longest x2 4.78 us: one_update(): jnp.einsum('crj,cd->drj', tri_normed, weight_out, preferred_element_type=...]
    convert_element_type x9 -> x0, local copies, waits for them, and re-layouts: 10.7 us -> none  [the longest x2 3.08 us: one_update(): (jax.nn.sigmoid(projected[2]) * projected[3] * pair_mask).astype(jnp.bflo...]
    reduce_sum x7 -> x0, other arithmetic: 7.83 us -> none  [the longest x4 5 us: layer_norm(): spread = jnp.mean(shifted * shifted, axis=axis_index, keepdims=True)]
  transfers between devices with their start and end apart: 6 -> 0, of which waited for: 6 -> 0; matrix products, arithmetic and copies ran while one was open for 1% -> 0% of each run, Pallas kernels for 0% -> 0%
where the time goes in v2:
time: 125 us
  Pallas kernels  119 us (95%)
  local copies, waits for them, and re-layouts  5.74 us (5%)
    pallas_call x1, Pallas kernels, on_device(): pl.pallas_call(kernel, out_shape=jax.ShapeDtypeStruct(pair.shape, BF16),...  119 us
    unnamed x13, local copies, waits for them, and re-layouts  5.74 us

profile of v2, /device:TPU:32, one launch (start us, length us, event | category | flops | bytes accessed | tf_op | source)
XLA Modules:
  0.0 125.0 jit_solution(4472881420547131238)
XLA Ops:
  0.0 0.0 copy-start.4
  0.0 0.7 copy-done.4
  0.7 0.0 copy-start
  0.7 1.1 copy-done
  1.7 0.0 copy-start.1
  1.7 1.0 copy-done.1
  2.7 0.0 copy-start.2
  2.7 0.8 copy-done.2
  3.6 0.0 copy-start.3
  3.6 0.7 copy-done.3
  4.2 0.0 copy-start.5
  4.2 0.7 copy-done.5
  4.9 119.2 %triangle.1 = bf16[12,192,128]{2,1,0:T(8,128)(2,1)S(1)} custom-call(bf16[12,192,128]{2,1,0:T(8,128)(2,1)S(1)} %copy-done, s32[768]{0:T(1024)S(1)} %copy-done.3, s32[6,128]{1,0:T(8,128)S(1)} %bitcast.1, f32[2,128]{1,0:T(2,128)S(1)} %copy-done.4, bf16[2,5,128,128]{3,2,1,0:T(8,128)(2,1)S(1)} %copy-done.1, f32[2,128]{1,0:T(2,128)S(1)} %copy-done.5, ...), custom_call_target="tpu_custom_call" | custom-call | tf_op jit(solution)/shard_map/triangle/pallas_call | solution.py:359
  124.2 0.8 copy.8
Async XLA Ops:
  0.0 0.7 copy-start.4
  0.7 1.1 copy-start
  1.7 1.0 copy-start.1
  2.7 0.8 copy-start.2
  3.6 0.7 copy-start.3
  4.2 0.7 copy-start.5

commit v3 on v2

--- a/solution.py
+++ b/solution.py
@@ -61,7 +61,6 @@
         load.start()
 
     lr0[1] = jnp.zeros(lr0.shape[1:], BF16)
-    lr1[...] = jnp.zeros_like(lr1)
 
     bits = [r // 2**k % 2 for k in range(4)]
 
@@ -70,17 +69,16 @@
         b1, b0 = 1 - step // 2, 1 - step % 2
         return 2 * ((zh // 2 + b1) % 2) + (zh % 2 + b0) % 2
 
-    def chips(g, last, visit):
-        @pl.loop(0, 4)
-        def _(hi):
-            b3, b2 = 1 - hi // 2, 1 - hi % 2
-            base = g * 16 + 8 * ((bits[3] + b3) % 2) + 4 * ((bits[2] + b2) % 2)
-            for low in range(7, -1, -1):
-                e = base
-                for k in range(2):
-                    e = e + 2**k * (1 - bits[k] if low >> (k + 1) & 1 else bits[k])
-                h = 1 - xhi if low & 1 else xhi
-                visit(e, h, low == 0 and last & (hi == 3))
+    def chips(g, z0, y0, step, visit):
+        mine = (step == CHUNKS - 1) & (bits[3] == z0) & (bits[0] == y0)
+        for low in range(7, -1, -1):
+            e = g * 16 + 8 * z0 + y0
+            e = e + 4 * (1 - bits[2] if low & 4 else bits[2])
+            e = e + 2 * (1 - bits[1] if low & 2 else bits[1])
+            h = 1 - xhi if low & 1 else xhi
+            visit(e, h, low == 0 and mine)
+
+    quarters = ((0, 0), (1, 1), (0, 1), (1, 0))
 
     barrier = pltpu.get_barrier_semaphore()
     pl.semaphore_signal(barrier, inc=1, device_id=partner, device_id_type=MESH)
@@ -96,7 +94,8 @@
             else:
                 pl.when(jnp.logical_not(mine))(signal)
 
-        chips(chunk_of(step), step == 3, greet)
+        for quarter in quarters:
+            chips(chunk_of(step), *quarter, step, greet)
 
     for load in loads:
         load.wait()
@@ -109,7 +108,7 @@
         gcol[u] = jnp.broadcast_to(out_gain[u : u + 1, :], (CH, CH)).T
 
     def norm(u):
-        @pl.loop(0, IL)
+        @pl.loop(0, IL, unroll=6)
         def _(i):
             val = zbuf[i]
             shifted = val.astype(F32) - dot(val, ones[...], NN) * (1.0 / CH)
@@ -117,7 +116,7 @@
             xn[i] = (shifted * lax.rsqrt(spread + 1e-05) * in_gain[u : u + 1, :]).astype(BF16)
 
     def gates(u):
-        @pl.loop(0, IL)
+        @pl.loop(0, IL, unroll=6)
         def _(i):
             gate[i] = sigmoid(dot(xn[i], w_in[u, 4], NN))
 
@@ -130,7 +129,7 @@
             zbuf[i, 320:384] = src[IL + i, tail_at]
 
     def project(u, g):
-        @pl.loop(0, IL)
+        @pl.loop(0, IL, unroll=6)
         def _(i):
             o = dot(wt[u, g], xn[i], NT)
             mask = pm[u, pl.ds(i, 1), :]
@@ -184,16 +183,8 @@
     pl.semaphore_wait(barrier, 128)
 
     for u in range(2):
-        @pl.loop(0, CHUNKS)
-        def _(step):
-            g = chunk_of(step)
-            if u == 0:
-                @pl.when(step > 0)
-                def _():
-                    project(u, g)
-            else:
-                project(u, g)
-
+        b_six = b.at[:, :, :, six, :]
+        for k in range(4):
             def post(e, h, mine):
                 if u == 0:
                     slot = lr0.at[:, :, xhi, r, six, :]
@@ -204,7 +195,14 @@
                     lr_send.at[u], lr_recv.at[u], (e, h * 2 + c), mine,
                 )
 
-            chips(g, step == 3, post)
+            @pl.loop(0, CHUNKS)
+            def _(step):
+                g = chunk_of(step)
+                if k == 0 and u == 0:
+                    pl.when(step > 0)(lambda: project(u, g))
+                elif k == 0:
+                    project(u, g)
+                chips(g, *quarters[k], step, post)
 
         if u == 0:
             swap = pltpu.make_async_remote_copy(
@@ -212,6 +210,7 @@
                 device_id=partner, device_id_type=MESH,
             )
             swap.start()
+            lr1[...] = jnp.zeros_like(lr1)
             turn(1)
             k_id = lax.broadcasted_iota(jnp.int32, (512, 384), 0)
             i_id = lax.broadcasted_iota(jnp.int32, (512, 384), 1)
@@ -236,9 +235,8 @@
         norm(u)
         gates(u)
 
-        whole = b.at[:, :, :, six, :]
+        pltpu.make_async_copy(b_six, b_six, lr_recv.at[u]).wait()
         most = b.at[pl.ds(0, CH - 1), :, :, six, :]
-        pltpu.make_async_copy(whole, whole, lr_recv.at[u]).wait()
         pltpu.make_async_copy(most, most, lr_send.at[u]).wait()
 
         if u == 0:
@@ -288,11 +286,17 @@
                 device_id=partner, device_id_type=MESH,
             )
 
-        @pl.loop(0, CHUNKS)
+        @pl.loop(0, CHUNKS, unroll=4)
         def _(step):
             n = chunk_of(step)
             xs[n] = product(1 - c, n).astype(BF16)
             give(n).start()
+
+        def back(e, h, mine):
+            send(
+                ts.at[e, h, :, six, :], tri.at[u, :, chip, six, :],
+                t_send.at[u], t_recv.at[u], (e, h * 2 + c), mine,
+            )
 
         @pl.loop(0, CHUNKS)
         def _(step):
@@ -315,21 +319,19 @@
                     tile = halves(low[:, cols], high[:, cols])
                     ts[at, h, 2] = tile.reshape(16, 8, 128).astype(BF16)
 
-            def post(e, h, mine):
-                send(
-                    ts.at[e, h, :, six, :], tri.at[u, :, chip, six, :],
-                    t_send.at[u], t_recv.at[u], (e, h * 2 + c), mine,
-                )
-
-            chips(n, step == 3, post)
+            chips(n, *quarters[0], step, back)
+
+        for k in range(1, 4):
+            @pl.loop(0, CHUNKS)
+            def _(step):
+                chips(chunk_of(step), *quarters[k], step, back)
 
         for n in range(CHUNKS):
             give(n).wait_send()
         whole = tri.at[u, :, :, six, :]
-        most = tri.at[u, :, pl.ds(0, CH - 1), six, :]
         pltpu.make_async_copy(whole, whole, t_recv.at[u]).wait()
 
-        @pl.loop(0, 3)
+        @pl.loop(0, 3, unroll=3)
         def _(k):
             tf[...] = tri[u, k].astype(F32).reshape(CH * 8, 128)
             at = pl.ds(pl.multiple_of(k * 128, 128), 128)
@@ -341,6 +343,7 @@
                 term = dot(normed, w_out[u], TN) * gate[i, at, :]
                 zbuf[i, at, :] = (zbuf[i, at, :].astype(F32) + term).astype(BF16)
 
+        most = tri.at[u, :, pl.ds(0, CH - 1), six, :]
         pltpu.make_async_copy(most, most, t_send.at[u]).wait()
         if u == 0:
             norm(1)
@@ -398,7 +401,7 @@
             dma((2,)), dma((2,)), dma((2,)), dma((2,)),
         ],
         compiler_params=pltpu.CompilerParams(
-            collective_id=0, has_side_effects=True, vmem_limit_bytes=48 * 2**20
+            collective_id=0, has_side_effects=True, vmem_limit_bytes=62 * 2**20
         ),
         name="triangle",
     )(pair, residue_mask, residue_mask.reshape(6, 128), in_gain, w_in, out_gain, w_out)

time: 125 us -> 113 us (0.904)
  Pallas kernels: 119 us -> 111 us
  local copies, waits for them, and re-layouts: 5.74 us -> 1.92 us
    pallas_call x1, Pallas kernels: 119 us -> 111 us  [on_device(): pl.pallas_call(kernel, out_shape=jax.ShapeDtypeStruct(pair.shape, BF16),...]
    unnamed x13 -> x1, local copies, waits for them, and re-layouts: 5.74 us -> 1.92 us
where the time goes in v3:
time: 113 us
  Pallas kernels  111 us (98%)
  local copies, waits for them, and re-layouts  1.92 us (2%)
    pallas_call x1, Pallas kernels, on_device(): pl.pallas_call(kernel, out_shape=jax.ShapeDtypeStruct(pair.shape, BF16),...  111 us

profile of v3, /device:TPU:32, one launch (start us, length us, event | category | flops | bytes accessed | tf_op | source)
XLA Modules:
  0.0 112.6 jit_solution(11203960104155388028)
XLA Ops:
  0.0 110.7 %triangle.1 = bf16[12,192,128]{2,1,0:T(8,128)(2,1)} custom-call(bf16[12,192,128]{2,1,0:T(8,128)(2,1)} %pair_hbm.1, s32[768]{0:T(1024)} %mask_hbm.1, s32[6,128]{1,0:T(8,128)} %bitcast.1, f32[2,128]{1,0:T(2,128)} %in_gain_hbm.1, bf16[2,5,128,128]{3,2,1,0:T(8,128)(2,1)} %w_in_hbm.1, f32[2,128]{1,0:T(2,128)} %out_gain_hbm.1, bf16[2,128,128]{2,1,0:T(8,128)(2,1)} %w_out_hbm.1), custom_call_target="tpu_custom_call" | custom-call | tf_op jit(solution)/shard_map/triangle/pallas_call | solution.py:362
  110.7 1.9 %copy.8 = bf16[12,192,128]{2,1,0:T(8,128)(2,1)} copy(bf16[12,192,128]{2,1,0:T(8,128)(2,1)} %triangle.1) | data formatting | bytes 1179648

commit v4 on v3

--- a/solution.py
+++ b/solution.py
@@ -12,6 +12,11 @@
 IL = 6
 CHUNKS = 4
 CW = CH // CHUNKS
+ORDER = (2, 3, 1, 0)
+FIXED = ("z0", "y0")
+GROUPS = ((0, 0), (1, 1), (0, 1), (1, 0))
+FREE = ("xhi", "y0", "y1", "xlo", "z0")
+STAGES = (((0, 1), (1, 2)), ((0, 3),))
 NT = (((1,), (1,)), ((), ()))
 NN = (((1,), (0,)), ((), ()))
 TN = (((0,), (0,)), ((), ()))
@@ -66,19 +71,27 @@
 
     def chunk_of(step):
         zh = r // 16
-        b1, b0 = 1 - step // 2, 1 - step % 2
-        return 2 * ((zh // 2 + b1) % 2) + (zh % 2 + b0) % 2
-
-    def chips(g, z0, y0, step, visit):
-        mine = (step == CHUNKS - 1) & (bits[3] == z0) & (bits[0] == y0)
-        for low in range(7, -1, -1):
-            e = g * 16 + 8 * z0 + y0
-            e = e + 4 * (1 - bits[2] if low & 4 else bits[2])
-            e = e + 2 * (1 - bits[1] if low & 2 else bits[1])
-            h = 1 - xhi if low & 1 else xhi
-            visit(e, h, low == 0 and mine)
-
-    quarters = ((0, 0), (1, 1), (0, 1), (1, 0))
+        flip = ORDER[-1]
+        for n in range(CHUNKS - 1):
+            flip = flip + jnp.where(step == n, ORDER[n] - ORDER[-1], 0)
+        return 2 * ((zh // 2 + flip // 2) % 2) + (zh % 2 + flip % 2) % 2
+
+    place = {"xhi": 1, "y0": 2, "y1": 4, "xlo": 8, "z0": 16}
+    here = dict(zip(place, [xhi] + bits))
+    free = [name for name in FREE if name not in FIXED]
+
+    def chips(g, group, step, visit):
+        mine = step == CHUNKS - 1
+        for name, value in zip(FIXED, group):
+            mine = mine & (here[name] == value)
+        for low in range(2 ** len(free) - 1, -1, -1):
+            to = dict(zip(FIXED, group))
+            for k, name in enumerate(free):
+                to[name] = 1 - here[name] if low >> k & 1 else here[name]
+            e = g * 16
+            for name in list(place)[1:]:
+                e = e + to[name] * (place[name] // 2)
+            visit(e, to["xhi"], low == 0 and mine)
 
     barrier = pltpu.get_barrier_semaphore()
     pl.semaphore_signal(barrier, inc=1, device_id=partner, device_id_type=MESH)
@@ -94,8 +107,8 @@
             else:
                 pl.when(jnp.logical_not(mine))(signal)
 
-        for quarter in quarters:
-            chips(chunk_of(step), *quarter, step, greet)
+        for group in GROUPS:
+            chips(chunk_of(step), group, step, greet)
 
     for load in loads:
         load.wait()
@@ -107,13 +120,15 @@
                 wt[u, g, v * CW : (v + 1) * CW, :] = turned[g * CW : (g + 1) * CW]
         gcol[u] = jnp.broadcast_to(out_gain[u : u + 1, :], (CH, CH)).T
 
-    def norm(u):
+    def norm(u, lo=0, n=3):
+        at = pl.ds(lo * 128, n * 128)
+
         @pl.loop(0, IL, unroll=6)
         def _(i):
-            val = zbuf[i]
+            val = zbuf[i, at]
             shifted = val.astype(F32) - dot(val, ones[...], NN) * (1.0 / CH)
             spread = dot((shifted * shifted).astype(BF16), ones[...], NN) * (1.0 / CH)
-            xn[i] = (shifted * lax.rsqrt(spread + 1e-05) * in_gain[u : u + 1, :]).astype(BF16)
+            xn[i, at] = (shifted * lax.rsqrt(spread + 1e-05) * in_gain[u : u + 1, :]).astype(BF16)
 
     def gates(u):
         @pl.loop(0, IL, unroll=6)
@@ -128,20 +143,22 @@
             zbuf[i, 256:320] = src[i, tail_at]
             zbuf[i, 320:384] = src[IL + i, tail_at]
 
-    def project(u, g):
+    def project(u, g, lo, n):
+        at = pl.ds(lo * 128, n * 128)
+
         @pl.loop(0, IL, unroll=6)
         def _(i):
-            o = dot(wt[u, g], xn[i], NT)
-            mask = pm[u, pl.ds(i, 1), :]
+            o = dot(wt[u, g], xn[i, at], NT)
+            mask = pm[u, pl.ds(i, 1), at]
             for s in range(2):
                 side = sigmoid(o[2 * s * CW : (2 * s + 1) * CW])
                 side = side * o[(2 * s + 1) * CW : (2 * s + 2) * CW] * mask
-                for k in range(3):
+                for k in range(n):
                     bf[s, k, pl.ds(i, CW, stride=8), :] = side[:, k * 128 : (k + 1) * 128]
 
         for s in range(2):
-            for k in range(3):
-                b[pl.ds(g * CW, CW), s, k] = bf[s, k].reshape(CW, 8, 128).astype(BF16)
+            for k in range(n):
+                b[pl.ds(g * CW, CW), s, lo + k] = bf[s, k].reshape(CW, 8, 128).astype(BF16)
 
     def send(src, dst, send_sem, recv_sem, to, mine):
         def remote():
@@ -178,20 +195,19 @@
     turn(0)
     to_own(pair)
     norm(0)
-    project(0, chunk_of(0))
+    project(0, chunk_of(0), 0, 3)
 
     pl.semaphore_wait(barrier, 128)
 
-    for u in range(2):
-        b_six = b.at[:, :, :, six, :]
-        for k in range(4):
+    def project_send(u, lo, n):
+        for k in range(len(GROUPS)):
             def post(e, h, mine):
                 if u == 0:
-                    slot = lr0.at[:, :, xhi, r, six, :]
+                    slot = lr0.at[:, pl.ds(lo, n), xhi, r, six, :]
                 else:
-                    slot = lr1.at[:, pl.ds(xhi * 3, 3), r, six, :]
+                    slot = lr1.at[:, pl.ds(xhi * 3 + lo, n), r, six, :]
                 send(
-                    b.at[e * 2 + h, :, :, six, :], slot,
+                    b.at[e * 2 + h, :, pl.ds(lo, n), six, :], slot,
                     lr_send.at[u], lr_recv.at[u], (e, h * 2 + c), mine,
                 )
 
@@ -199,10 +215,26 @@
             def _(step):
                 g = chunk_of(step)
                 if k == 0 and u == 0:
-                    pl.when(step > 0)(lambda: project(u, g))
+                    pl.when(step > 0)(lambda: project(u, g, lo, n))
                 elif k == 0:
-                    project(u, g)
-                chips(g, *quarters[k], step, post)
+                    project(u, g, lo, n)
+                chips(g, GROUPS[k], step, post)
+
+    def finish(u, lo, n):
+        for k in range(lo, lo + n):
+            tf[...] = tri[u, k].astype(F32).reshape(CH * 8, 128)
+            at = pl.ds(k * 128, 128)
+            for i in range(IL):
+                val = tf[pl.ds(i, CH, stride=8), :]
+                shifted = val - jnp.mean(val, axis=0, keepdims=True)
+                spread = jnp.mean(shifted * shifted, axis=0, keepdims=True)
+                normed = (shifted * lax.rsqrt(spread + 1e-05) * gcol[u]).astype(BF16)
+                term = dot(normed, w_out[u], TN) * gate[i, at, :]
+                zbuf[i, at, :] = (zbuf[i, at, :].astype(F32) + term).astype(BF16)
+
+    for u in range(2):
+        if u == 0:
+            project_send(0, 0, 3)
 
         if u == 0:
             swap = pltpu.make_async_remote_copy(
@@ -235,6 +267,7 @@
         norm(u)
         gates(u)
 
+        b_six = b.at[:, :, :, six, :]
         pltpu.make_async_copy(b_six, b_six, lr_recv.at[u]).wait()
         most = b.at[pl.ds(0, CH - 1), :, :, six, :]
         pltpu.make_async_copy(most, most, lr_send.at[u]).wait()
@@ -292,11 +325,16 @@
             xs[n] = product(1 - c, n).astype(BF16)
             give(n).start()
 
-        def back(e, h, mine):
-            send(
-                ts.at[e, h, :, six, :], tri.at[u, :, chip, six, :],
-                t_send.at[u], t_recv.at[u], (e, h * 2 + c), mine,
-            )
+        def back(stage):
+            lo, n = STAGES[u][stage]
+
+            def post(e, h, mine):
+                send(
+                    ts.at[e, h, pl.ds(lo, n), six, :], tri.at[u, pl.ds(lo, n), chip, six, :],
+                    t_send.at[u], t_recv.at[u, stage], (e, h * 2 + c), mine,
+                )
+
+            return post
 
         @pl.loop(0, CHUNKS)
         def _(step):
@@ -319,34 +357,25 @@
                     tile = halves(low[:, cols], high[:, cols])
                     ts[at, h, 2] = tile.reshape(16, 8, 128).astype(BF16)
 
-            chips(n, *quarters[0], step, back)
-
-        for k in range(1, 4):
-            @pl.loop(0, CHUNKS)
-            def _(step):
-                chips(chunk_of(step), *quarters[k], step, back)
+            chips(n, GROUPS[0], step, back(0))
+
+        for stage in range(len(STAGES[u])):
+            for k in range(0 if stage else 1, len(GROUPS)):
+                @pl.loop(0, CHUNKS)
+                def _(step):
+                    chips(chunk_of(step), GROUPS[k], step, back(stage))
 
         for n in range(CHUNKS):
             give(n).wait_send()
-        whole = tri.at[u, :, :, six, :]
-        pltpu.make_async_copy(whole, whole, t_recv.at[u]).wait()
-
-        @pl.loop(0, 3, unroll=3)
-        def _(k):
-            tf[...] = tri[u, k].astype(F32).reshape(CH * 8, 128)
-            at = pl.ds(pl.multiple_of(k * 128, 128), 128)
-            for i in range(IL):
-                val = tf[pl.ds(i, CH, stride=8), :]
-                shifted = val - jnp.mean(val, axis=0, keepdims=True)
-                spread = jnp.mean(shifted * shifted, axis=0, keepdims=True)
-                normed = (shifted * lax.rsqrt(spread + 1e-05) * gcol[u]).astype(BF16)
-                term = dot(normed, w_out[u], TN) * gate[i, at, :]
-                zbuf[i, at, :] = (zbuf[i, at, :].astype(F32) + term).astype(BF16)
-
+        for stage, (lo, n) in enumerate(STAGES[u]):
+            part = tri.at[u, pl.ds(lo, n), :, six, :]
+            pltpu.make_async_copy(part, part, t_recv.at[u, stage]).wait()
+            finish(u, lo, n)
+            if u == 0:
+                norm(1, lo, n)
+                project_send(1, lo, n)
         most = tri.at[u, :, pl.ds(0, CH - 1), six, :]
         pltpu.make_async_copy(most, most, t_send.at[u]).wait()
-        if u == 0:
-            norm(1)
 
     @pl.loop(0, IL)
     def _(i):
@@ -398,7 +427,7 @@
             pltpu.VMEM((2, 8, 384), F32),
             pltpu.VMEM((CH, 128), BF16),
             dma((7,)), dma((2,)), dma((2,)), dma((2, 4)), dma((2, 4)),
-            dma((2,)), dma((2,)), dma((2,)), dma((2,)),
+            dma((2,)), dma((2,)), dma((2,)), dma((2, 2)),
         ],
         compiler_params=pltpu.CompilerParams(
             collective_id=0, has_side_effects=True, vmem_limit_bytes=62 * 2**20

time: 113 us -> 107 us (0.947)
  Pallas kernels: 111 us -> 105 us
    pallas_call x1, Pallas kernels: 111 us -> 105 us  [on_device(): pl.pallas_call(kernel, out_shape=jax.ShapeDtypeStruct(pair.shape, BF16),...]
where the time goes in v4:
time: 107 us
  Pallas kernels  105 us (98%)
  local copies, waits for them, and re-layouts  1.92 us (2%)
    pallas_call x1, Pallas kernels, on_device(): pl.pallas_call(kernel, out_shape=jax.ShapeDtypeStruct(pair.shape, BF16),...  105 us

profile of v4, /device:TPU:32, one launch (start us, length us, event | category | flops | bytes accessed | tf_op | source)
XLA Modules:
  0.0 107.2 jit_solution(16109905632517048113)
XLA Ops:
  0.0 105.2 %triangle.1 = bf16[12,192,128]{2,1,0:T(8,128)(2,1)} custom-call(bf16[12,192,128]{2,1,0:T(8,128)(2,1)} %pair_hbm.1, s32[768]{0:T(1024)} %mask_hbm.1, s32[6,128]{1,0:T(8,128)} %bitcast.1, f32[2,128]{1,0:T(2,128)} %in_gain_hbm.1, bf16[2,5,128,128]{3,2,1,0:T(8,128)(2,1)} %w_in_hbm.1, f32[2,128]{1,0:T(2,128)} %out_gain_hbm.1, bf16[2,128,128]{2,1,0:T(8,128)(2,1)} %w_out_hbm.1), custom_call_target="tpu_custom_call" | custom-call | tf_op jit(solution)/shard_map/triangle/pallas_call | solution.py:391
  105.3 1.9 %copy.8 = bf16[12,192,128]{2,1,0:T(8,128)(2,1)} copy(bf16[12,192,128]{2,1,0:T(8,128)(2,1)} %triangle.1) | data formatting | bytes 1179648

commit v5 on v4

--- a/solution.py
+++ b/solution.py
@@ -16,7 +16,7 @@
 FIXED = ("z0", "y0")
 GROUPS = ((0, 0), (1, 1), (0, 1), (1, 0))
 FREE = ("xhi", "y0", "y1", "xlo", "z0")
-STAGES = (((0, 1), (1, 2)), ((0, 3),))
+STAGES = (((0, 1), (1, 2)), ((0, 2), (2, 1)))
 NT = (((1,), (1,)), ((), ()))
 NN = (((1,), (0,)), ((), ()))
 TN = (((0,), (0,)), ((), ()))
@@ -37,7 +37,7 @@
 def kernel(
     pair_hbm, mask_hbm, mask6_hbm, in_gain_hbm, w_in_hbm, out_gain_hbm, w_out_hbm, out_ref,
     pair, mask_s, mask_v, in_gain, w_in, out_gain, w_out,
-    zin, zbuf, zown, xn, gate, wt, bf, b, lr0, lr1, rc, lt, tl, sel, selt, xs0, xp0, xs1, xp1,
+    zin, zbuf, zown, xn, gate, wt, bf, b, lr0, lr1, rc, lt, tl, sel, selt, xs0, xp0, xs1, xp1, xst, xpt,
     ts, tri, tf, gcol, pm, ones,
     in_sem, x_send, x_recv, p_send, p_recv, lr_send, lr_recv, t_send, t_recv,
 ):
@@ -79,19 +79,19 @@
     place = {"xhi": 1, "y0": 2, "y1": 4, "xlo": 8, "z0": 16}
     here = dict(zip(place, [xhi] + bits))
     free = [name for name in FREE if name not in FIXED]
+    offsets = []
+    for low in range(2 ** len(free) - 1, -1, -1):
+        to = {name: 1 - here[name] if low >> k & 1 else here[name] for k, name in enumerate(free)}
+        e = sum(to[name] * (place[name] // 2) for name in free if name != "xhi")
+        offsets.append((low, e, to["xhi"]))
 
     def chips(g, group, step, visit):
         mine = step == CHUNKS - 1
         for name, value in zip(FIXED, group):
             mine = mine & (here[name] == value)
-        for low in range(2 ** len(free) - 1, -1, -1):
-            to = dict(zip(FIXED, group))
-            for k, name in enumerate(free):
-                to[name] = 1 - here[name] if low >> k & 1 else here[name]
-            e = g * 16
-            for name in list(place)[1:]:
-                e = e + to[name] * (place[name] // 2)
-            visit(e, to["xhi"], low == 0 and mine)
+        base = g * 16 + sum(value * (place[name] // 2) for name, value in zip(FIXED, group))
+        for low, e, h in offsets:
+            visit(base + e, h, low == 0 and mine)
 
     barrier = pltpu.get_barrier_semaphore()
     pl.semaphore_signal(barrier, inc=1, device_id=partner, device_id_type=MESH)
@@ -199,26 +199,29 @@
 
     pl.semaphore_wait(barrier, 128)
 
-    def project_send(u, lo, n):
-        for k in range(len(GROUPS)):
-            def post(e, h, mine):
-                if u == 0:
-                    slot = lr0.at[:, pl.ds(lo, n), xhi, r, six, :]
-                else:
-                    slot = lr1.at[:, pl.ds(xhi * 3 + lo, n), r, six, :]
-                send(
-                    b.at[e * 2 + h, :, pl.ds(lo, n), six, :], slot,
-                    lr_send.at[u], lr_recv.at[u], (e, h * 2 + c), mine,
-                )
-
-            @pl.loop(0, CHUNKS)
-            def _(step):
-                g = chunk_of(step)
-                if k == 0 and u == 0:
-                    pl.when(step > 0)(lambda: project(u, g, lo, n))
-                elif k == 0:
-                    project(u, g, lo, n)
-                chips(g, GROUPS[k], step, post)
+    def project_send(u, lo, n, stage, parts):
+        for turn, (side, sides) in enumerate(((0, 1), (1, 1)) if stage == 2 else ((0, 2),)):
+            sides = pl.ds(side, sides)
+
+            for k in range(len(GROUPS)):
+                def post(e, h, mine):
+                    if u == 0:
+                        slot = lr0.at[sides, pl.ds(lo, n), xhi, r, six, :]
+                    else:
+                        slot = lr1.at[sides, pl.ds(xhi * 3 + lo, n), r, six, :]
+                    send(
+                        b.at[e * 2 + h, sides, pl.ds(lo, n), six, :], slot,
+                        lr_send.at[u], lr_recv.at[u, stage + turn], (e, h * 2 + c), mine,
+                    )
+
+                @pl.loop(0, CHUNKS)
+                def _(step):
+                    g = chunk_of(step)
+                    if k == 0 and turn == 0 and u == 0:
+                        pl.when(step > 0)(lambda: project(u, g, *parts))
+                    elif k == 0 and turn == 0 and parts:
+                        project(u, g, *parts)
+                    chips(g, GROUPS[k], step, post)
 
     def finish(u, lo, n):
         for k in range(lo, lo + n):
@@ -232,9 +235,17 @@
                 term = dot(normed, w_out[u], TN) * gate[i, at, :]
                 zbuf[i, at, :] = (zbuf[i, at, :].astype(F32) + term).astype(BF16)
 
+    def lr_sent(u):
+        most = b.at[pl.ds(0, CH - 1), :, :, six, :]
+        pltpu.make_async_copy(most, most, lr_send.at[u]).wait()
+
+    def t_sent(u):
+        most = tri.at[u, :, pl.ds(0, CH - 1), six, :]
+        pltpu.make_async_copy(most, most, t_send.at[u]).wait()
+
     for u in range(2):
         if u == 0:
-            project_send(0, 0, 3)
+            project_send(0, 0, 3, 0, (0, 3))
 
         if u == 0:
             swap = pltpu.make_async_remote_copy(
@@ -267,10 +278,15 @@
         norm(u)
         gates(u)
 
-        b_six = b.at[:, :, :, six, :]
-        pltpu.make_async_copy(b_six, b_six, lr_recv.at[u]).wait()
-        most = b.at[pl.ds(0, CH - 1), :, :, six, :]
-        pltpu.make_async_copy(most, most, lr_send.at[u]).wait()
+        def received(stage, ref):
+            pltpu.make_async_copy(ref, ref, lr_recv.at[u, stage]).wait()
+
+        if u == 0:
+            received(0, b.at[:, :, :, six, :])
+        else:
+            for stage in range(3):
+                received(stage, b.at[:, 0 : 1 if stage == 2 else 2, 0, six, :])
+
 
         if u == 0:
             xs, xp = xs0, xp0
@@ -303,19 +319,22 @@
                 turned = dot(sel[...], jnp.concatenate(part, axis=1), NT).astype(BF16)
                 for d in range(2):
                     lt[d, half * 256 : half * 256 + 256] = turned[d * 256 : d * 256 + 256]
-            t0, t1 = lr1[1, 1].reshape(512, 128), lr1[1, 4].reshape(512, 128)
-            tl[0, 0] = halves(t0[:, :64], t1[:, :64])
-            tl[0, 1] = halves(t0[:, 64:], t1[:, 64:])
-
             def product(d, n):
                 at = pl.ds(pl.multiple_of(n * 128, 128), 128)
                 left = jnp.concatenate([lt[0, at], lt[1, at]], axis=0)
                 right = [lr1[1, h * 3 + 2 * d].reshape(512, 128) for h in range(2)]
-                return dot(left, jnp.concatenate(right + [tl[0, d]], axis=1), NN)
-
-        def give(n):
+                return dot(left, jnp.concatenate(right, axis=1), NN)
+
+            def product_tail(d, n):
+                at = pl.ds(pl.multiple_of(n * 128, 128), 128)
+                left = jnp.concatenate([lt[0, at], lt[1, at]], axis=0)
+                return dot(left, tl[0, d], NN)
+
+        def give(n, tail=False):
+            here, there = (xst, xpt) if tail else (xs, xp)
+            row = 2 if tail else u
             return pltpu.make_async_remote_copy(
-                xs.at[n], xp.at[n], p_send.at[u, n], p_recv.at[u, n],
+                here.at[n], there.at[n], p_send.at[row, n], p_recv.at[row, n],
                 device_id=partner, device_id_type=MESH,
             )
 
@@ -335,6 +354,9 @@
                 )
 
             return post
+
+        if u == 1:
+            t_sent(0)
 
         @pl.loop(0, CHUNKS)
         def _(step):
@@ -351,31 +373,66 @@
             else:
                 low, high = p[0:128], p[128:256]
                 for h in range(2):
-                    cols = slice(256 + h * 64, 320 + h * 64)
                     ts[at, h, 0] = low[:, h * 128 : h * 128 + 128].reshape(16, 8, 128).astype(BF16)
                     ts[at, h, 1] = high[:, h * 128 : h * 128 + 128].reshape(16, 8, 128).astype(BF16)
+
+            for group in GROUPS[:4]:
+                chips(n, group, step, back(0))
+
+        for k in range(4, len(GROUPS)):
+            @pl.loop(0, CHUNKS)
+            def _(step):
+                chips(chunk_of(step), GROUPS[k], step, back(0))
+
+        if u == 1:
+            received(3, b.at[:, 0:1, 0, six, :])
+            t0, t1 = lr1[1, 1].reshape(512, 128), lr1[1, 4].reshape(512, 128)
+            tl[0, 0] = halves(t0[:, :64], t1[:, :64])
+            tl[0, 1] = halves(t0[:, 64:], t1[:, 64:])
+
+            @pl.loop(0, CHUNKS, unroll=4)
+            def _(step):
+                n = chunk_of(step)
+                xst[n] = product_tail(1 - c, n).astype(BF16)
+                give(n, True).start()
+
+            @pl.loop(0, CHUNKS)
+            def _(step):
+                n = chunk_of(step)
+                p = product_tail(c, n)
+                give(n, True).wait_recv()
+                p = p + xpt[n].astype(F32)
+                low, high = p[0:128], p[128:256]
+                for h in range(2):
+                    cols = slice(h * 64, h * 64 + 64)
                     tile = halves(low[:, cols], high[:, cols])
-                    ts[at, h, 2] = tile.reshape(16, 8, 128).astype(BF16)
-
-            chips(n, GROUPS[0], step, back(0))
-
-        for stage in range(len(STAGES[u])):
-            for k in range(0 if stage else 1, len(GROUPS)):
+                    ts[pl.ds(n * 16, 16), h, 2] = tile.reshape(16, 8, 128).astype(BF16)
+
+        for stage in range(1, len(STAGES[u])):
+            for k in range(len(GROUPS)):
                 @pl.loop(0, CHUNKS)
                 def _(step):
                     chips(chunk_of(step), GROUPS[k], step, back(stage))
 
         for n in range(CHUNKS):
             give(n).wait_send()
+            if u == 1:
+                give(n, True).wait_send()
         for stage, (lo, n) in enumerate(STAGES[u]):
             part = tri.at[u, pl.ds(lo, n), :, six, :]
             pltpu.make_async_copy(part, part, t_recv.at[u, stage]).wait()
             finish(u, lo, n)
             if u == 0:
                 norm(1, lo, n)
-                project_send(1, lo, n)
-        most = tri.at[u, :, pl.ds(0, CH - 1), six, :]
-        pltpu.make_async_copy(most, most, t_send.at[u]).wait()
+                if stage == 0:
+                    lr_sent(0)
+                if stage == 0:
+                    project_send(1, 0, 1, 0, (0, 1))
+                else:
+                    project_send(1, 2, 1, 1, (1, 2))
+                    project_send(1, 1, 1, 2, None)
+    lr_sent(1)
+    t_sent(1)
 
     @pl.loop(0, IL)
     def _(i):
@@ -418,16 +475,18 @@
             pltpu.VMEM((384, 512), BF16),
             pltpu.VMEM((4, 128, 768), BF16),
             pltpu.VMEM((4, 128, 768), BF16),
-            pltpu.VMEM((4, 256, 384), BF16),
-            pltpu.VMEM((4, 256, 384), BF16),
+            pltpu.VMEM((4, 256, 256), BF16),
+            pltpu.VMEM((4, 256, 256), BF16),
+            pltpu.VMEM((4, 256, 128), BF16),
+            pltpu.VMEM((4, 256, 128), BF16),
             pltpu.VMEM((64, 2, 3, 8, 128), BF16),
             pltpu.VMEM((2, 3, CH, 8, 128), BF16),
             pltpu.VMEM((CH * 8, 128), F32),
             pltpu.VMEM((2, CH, 128), F32),
             pltpu.VMEM((2, 8, 384), F32),
             pltpu.VMEM((CH, 128), BF16),
-            dma((7,)), dma((2,)), dma((2,)), dma((2, 4)), dma((2, 4)),
-            dma((2,)), dma((2,)), dma((2,)), dma((2, 2)),
+            dma((7,)), dma((2,)), dma((2,)), dma((3, 4)), dma((3, 4)),
+            dma((2,)), dma((2, 4)), dma((2,)), dma((2, 3)),
         ],
         compiler_params=pltpu.CompilerParams(
             collective_id=0, has_side_effects=True, vmem_limit_bytes=62 * 2**20

time: 107 us -> 105 us (0.981)
  Pallas kernels: 105 us -> 103 us
    pallas_call x1, Pallas kernels: 105 us -> 103 us  [on_device(): pl.pallas_call(kernel, out_shape=jax.ShapeDtypeStruct(pair.shape, BF16),...]
where the time goes in v5:
time: 105 us
  Pallas kernels  103 us (98%)
  local copies, waits for them, and re-layouts  1.92 us (2%)
    pallas_call x1, Pallas kernels, on_device(): pl.pallas_call(kernel, out_shape=jax.ShapeDtypeStruct(pair.shape, BF16),...  103 us

profile of v5, /device:TPU:32, one launch (start us, length us, event | category | flops | bytes accessed | tf_op | source)
XLA Modules:
  0.0 105.2 jit_solution(2329273625935382037)
XLA Ops:
  0.0 103.3 %triangle.1 = bf16[12,192,128]{2,1,0:T(8,128)(2,1)} custom-call(bf16[12,192,128]{2,1,0:T(8,128)(2,1)} %pair_hbm.1, s32[768]{0:T(1024)} %mask_hbm.1, s32[6,128]{1,0:T(8,128)} %bitcast.1, f32[2,128]{1,0:T(2,128)} %in_gain_hbm.1, bf16[2,5,128,128]{3,2,1,0:T(8,128)(2,1)} %w_in_hbm.1, f32[2,128]{1,0:T(2,128)} %out_gain_hbm.1, bf16[2,128,128]{2,1,0:T(8,128)(2,1)} %w_out_hbm.1), custom_call_target="tpu_custom_call" | custom-call | tf_op jit(solution)/shard_map/triangle/pallas_call | solution.py:448
  103.3 1.9 %copy.8 = bf16[12,192,128]{2,1,0:T(8,128)(2,1)} copy(bf16[12,192,128]{2,1,0:T(8,128)(2,1)} %triangle.1) | data formatting | bytes 1179648

commit v6 on v5

--- a/solution.py
+++ b/solution.py
@@ -195,7 +195,9 @@
     turn(0)
     to_own(pair)
     norm(0)
-    project(0, chunk_of(0), 0, 3)
+    @pl.loop(0, CHUNKS)
+    def _(step):
+        project(0, chunk_of(step), 0, 3)
 
     pl.semaphore_wait(barrier, 128)
 
@@ -217,9 +219,7 @@
                 @pl.loop(0, CHUNKS)
                 def _(step):
                     g = chunk_of(step)
-                    if k == 0 and turn == 0 and u == 0:
-                        pl.when(step > 0)(lambda: project(u, g, *parts))
-                    elif k == 0 and turn == 0 and parts:
+                    if k == 0 and turn == 0 and u == 1 and parts:
                         project(u, g, *parts)
                     chips(g, GROUPS[k], step, post)
 

time: 105 us -> 105 us (level)
  no operation moved by 1% of the time
where the time goes in v6:
time: 105 us
  Pallas kernels  103 us (98%)
  local copies, waits for them, and re-layouts  1.92 us (2%)
    pallas_call x1, Pallas kernels, on_device(): pl.pallas_call(kernel, out_shape=jax.ShapeDtypeStruct(pair.shape, BF16),...  103 us

profile of v6, /device:TPU:32, one launch (start us, length us, event | category | flops | bytes accessed | tf_op | source)
XLA Modules:
  0.0 104.6 jit_solution(16150823721381974660)
XLA Ops:
  0.0 102.7 %triangle.1 = bf16[12,192,128]{2,1,0:T(8,128)(2,1)} custom-call(bf16[12,192,128]{2,1,0:T(8,128)(2,1)} %pair_hbm.1, s32[768]{0:T(1024)} %mask_hbm.1, s32[6,128]{1,0:T(8,128)} %bitcast.1, f32[2,128]{1,0:T(2,128)} %in_gain_hbm.1, bf16[2,5,128,128]{3,2,1,0:T(8,128)(2,1)} %w_in_hbm.1, f32[2,128]{1,0:T(2,128)} %out_gain_hbm.1, bf16[2,128,128]{2,1,0:T(8,128)(2,1)} %w_out_hbm.1), custom_call_target="tpu_custom_call" | custom-call | tf_op jit(solution)/shard_map/triangle/pallas_call | solution.py:448
  102.7 1.9 %copy.8 = bf16[12,192,128]{2,1,0:T(8,128)(2,1)} copy(bf16[12,192,128]{2,1,0:T(8,128)(2,1)} %triangle.1) | data formatting | bytes 1179648
